TPU v7x, 32 devices: a whole 2x2x4 slice. The times are simulated.
32 devices in a mesh: seq: 4 (over z), dp: 8 (over y, x, core).
Axes of the slice: x: 2, y: 2, z: 4, core: 2. Of those that a mesh axis runs over, the one named last changes fastest.
Arguments:
- tokens: bfloat16 [8, 1024, 768], P('dp', 'seq'), may hold values from -6 to 6
- qkv_weight: bfloat16 [768, 2304], P('dp'), may hold values from -0.21875 to 0.21875
- proj_weight: bfloat16 [768, 768], P('dp'), may hold values from -0.875 to 0.875
- hidden_weight: bfloat16 [768, 3072], P('dp'), may hold values from -0.21875 to 0.21875
- output_weight: bfloat16 [3072, 768], P('dp'), may hold values from -0.109375 to 0.109375
- first_gain: bfloat16 [768], P('dp'), may hold values from 0.25 to 1.75
- first_bias: bfloat16 [768], P('dp'), may hold values from -2.5 to 2.5
- second_gain: bfloat16 [768], P('dp'), may hold values from 0.25 to 1.75
- second_bias: bfloat16 [768], P('dp'), may hold values from -2.5 to 2.5
- cotangent: bfloat16 [8, 1024, 768], P('dp', 'seq'), may hold values from -6 to 6
Outputs:
- block_out: bfloat16 [8, 1024, 768], P('dp', 'seq')
- tokens_gradient: bfloat16 [8, 1024, 768], P('dp', 'seq')
- qkv_gradient: float32 [768, 2304], P('dp')
- proj_gradient: float32 [768, 768], P('dp')
- hidden_gradient: float32 [768, 3072], P('dp')
- output_gradient: float32 [3072, 768], P('dp')
- first_gain_gradient: float32 [768], P('dp')
- first_bias_gradient: float32 [768], P('dp')
- second_gain_gradient: float32 [768], P('dp')
- second_bias_gradient: float32 [768], P('dp')
All inputs are finite; a program needn't handle non-finite values.
Results may differ from a plain program's by a relative error of at most 0.012.
Values may be sent and summed in bfloat16 or wider, within the bound.
A program may use at most 256 MiB of HBM per device.

v0:
```python
import jax
import jax.numpy as jnp
from jax import lax
from jax.sharding import PartitionSpec as P

HEAD_DIM = 64
LOW = jnp.bfloat16
F32 = jnp.float32


def layer_norm(values, gain, bias):
    average = jnp.mean(values, -1, keepdims=True)
    centred = values - average
    variance = jnp.mean(centred * centred, -1, keepdims=True)
    return centred * lax.rsqrt(variance + 1e-05) * gain + bias


def gelu_tanh(values):
    return jax.nn.gelu(values, approximate=True)


def matmul(left, right):
    return jnp.dot(left, right, preferred_element_type=F32)


def matmul_left_t(left, right):
    return lax.dot_general(left, right, (((0,), (0,)), ((), ())), preferred_element_type=F32)


def matmul_right_t(left, right):
    return lax.dot_general(left, right, (((1,), (1,)), ((), ())), preferred_element_type=F32)


def gather_seq(value):
    return lax.all_gather(value, "seq", axis=0, tiled=True)


def scatter_seq(value):
    return lax.psum_scatter(value.astype(LOW), "seq", scatter_dimension=0, tiled=True).astype(F32)


def attention_forward(queries, keys, values):
    length, local_width = queries.shape
    heads_here = local_width // HEAD_DIM
    block_rows = min(512, length)
    blocks = length // block_rows
    scale = HEAD_DIM ** (-0.5)
    outs, logs = ([], [])
    key_index = jnp.arange(length)
    for b in range(blocks):
        seen = (b + 1) * block_rows
        q = queries[b * block_rows : seen].reshape(block_rows, heads_here, HEAD_DIM)
        k = keys[:seen].reshape(seen, heads_here, HEAD_DIM)
        v = values[:seen].reshape(seen, heads_here, HEAD_DIM)
        raw = jnp.einsum("qhd,khd->hqk", q, k, preferred_element_type=F32)
        positions = b * block_rows + jnp.arange(block_rows)
        causal = key_index[None, :seen] <= positions[:, None]
        scores = jnp.where(causal[None], raw * scale, -1e30)
        largest = jnp.max(scores, -1, keepdims=True)
        expo = jnp.exp(scores - largest)
        total = jnp.sum(expo, -1, keepdims=True)
        probs = (expo / total).astype(LOW)
        context = jnp.einsum("hqk,khd->qhd", probs, v, preferred_element_type=F32)
        outs.append(context.astype(LOW).reshape(block_rows, local_width))
        logs.append(largest + jnp.log(total))
    return (jnp.concatenate(outs, axis=0), logs)


def attention_backward(queries, keys, values, grads, logs):
    length, local_width = queries.shape
    heads_here = local_width // HEAD_DIM
    block_rows = min(512, length)
    blocks = length // block_rows
    scale = HEAD_DIM ** (-0.5)
    key_index = jnp.arange(length)
    query_grads = []
    key_sum = jnp.zeros((length, heads_here, HEAD_DIM), F32)
    value_sum = jnp.zeros((length, heads_here, HEAD_DIM), F32)
    for b in range(blocks):
        seen = (b + 1) * block_rows
        q = queries[b * block_rows : seen].reshape(block_rows, heads_here, HEAD_DIM)
        g = grads[b * block_rows : seen].reshape(block_rows, heads_here, HEAD_DIM)
        k = keys[:seen].reshape(seen, heads_here, HEAD_DIM)
        v = values[:seen].reshape(seen, heads_here, HEAD_DIM)
        raw = jnp.einsum("qhd,khd->hqk", q, k, preferred_element_type=F32)
        positions = b * block_rows + jnp.arange(block_rows)
        causal = key_index[None, :seen] <= positions[:, None]
        scores = jnp.where(causal[None], raw * scale, -1e30)
        probs = jnp.exp(scores - logs[b])
        low_probs = probs.astype(LOW)
        value_term = jnp.einsum("hqk,qhd->khd", low_probs, g, preferred_element_type=F32)
        prob_grad = jnp.einsum("qhd,khd->hqk", g, v, preferred_element_type=F32)
        score_grad = (probs * (prob_grad - jnp.sum(probs * prob_grad, -1, keepdims=True))).astype(
            LOW
        )
        query_grad = jnp.einsum("hqk,khd->qhd", score_grad, k, preferred_element_type=F32) * scale
        key_term = jnp.einsum("hqk,qhd->khd", score_grad, q, preferred_element_type=F32) * scale
        pad = ((0, length - seen), (0, 0), (0, 0))
        key_sum = key_sum + jnp.pad(key_term, pad)
        value_sum = value_sum + jnp.pad(value_term, pad)
        query_grads.append(query_grad.astype(LOW).reshape(block_rows, local_width))
    return (
        jnp.concatenate(query_grads, axis=0),
        key_sum.astype(LOW).reshape(length, local_width),
        value_sum.astype(LOW).reshape(length, local_width),
    )


def on_device(
    tokens,
    qkv_weight,
    proj_weight,
    hidden_weight,
    output_weight,
    first_gain,
    first_bias,
    second_gain,
    second_bias,
    cotangent,
):
    parts = lax.axis_size("seq")
    groups = lax.axis_size("dp")
    part = lax.axis_index("seq")
    inputs_low = tokens[0]
    rows, width = inputs_low.shape
    model_rows = qkv_weight.shape[0]
    local_width = width // parts
    hidden_rows = output_weight.shape[0] // parts
    hidden_here = hidden_rows * groups
    qkv_here = lax.dynamic_index_in_dim(
        qkv_weight.reshape(model_rows, 3, parts, local_width), part, 2, keepdims=False
    ).reshape(model_rows, 3 * local_width)
    hidden_cols = lax.dynamic_index_in_dim(
        hidden_weight.reshape(model_rows, groups, parts, hidden_rows), part, 2, keepdims=False
    ).reshape(model_rows, hidden_here)
    output_here = lax.dynamic_slice_in_dim(output_weight, part * hidden_rows, hidden_rows, 0)
    norms = jnp.stack([first_gain, first_bias, second_gain, second_bias], axis=0)
    norms = lax.all_gather(norms, "dp", axis=1, tiled=True).astype(F32)
    gain_one, bias_one, gain_two, bias_two = (norms[0], norms[1], norms[2], norms[3])
    all_tokens = gather_seq(inputs_low)
    wide_qkv = lax.all_gather(qkv_here, "dp", axis=0, tiled=True)
    wide_proj = lax.all_gather(proj_weight, "dp", axis=0, tiled=True)
    wide_hidden = lax.all_gather(hidden_cols, "dp", axis=0, tiled=True)
    wide_output = lax.all_gather(output_here, "dp", axis=0, tiled=True)
    all_grads = gather_seq(cotangent[0])
    inputs = all_tokens.astype(F32)
    lowered_one = layer_norm(inputs, gain_one, bias_one).astype(LOW)
    projected = matmul(lowered_one, wide_qkv).astype(LOW)
    queries = projected[:, :local_width]
    keys = projected[:, local_width : 2 * local_width]
    values = projected[:, 2 * local_width :]
    context_here, logs = attention_forward(queries, keys, values)
    context = lax.all_gather(context_here, "seq", axis=1, tiled=True)
    middle = inputs + matmul(context, wide_proj)
    lowered_two = layer_norm(middle, gain_two, bias_two).astype(LOW)
    hidden_pre = matmul(lowered_two, wide_hidden)
    activated_float, gelu_pull = jax.vjp(gelu_tanh, hidden_pre)
    activated = activated_float.astype(LOW)
    act_grad = matmul_right_t(all_grads, wide_output)
    pre_grad = gelu_pull(act_grad)[0].astype(LOW)
    normed_two_grad = scatter_seq(matmul_right_t(pre_grad, wide_hidden))
    ffn_out = scatter_seq(matmul(activated, wide_output))
    middle_own = lax.dynamic_slice_in_dim(middle, part * rows, rows, 0)
    block_out = middle_own + ffn_out
    _, norm_pull_two = jax.vjp(layer_norm, middle_own, gain_two, bias_two)
    middle_part, gain_two_term, bias_two_term = norm_pull_two(normed_two_grad)
    middle_grad = cotangent[0].astype(F32) + middle_part
    attn_grad = gather_seq(middle_grad.astype(LOW))
    proj_here = lax.dynamic_slice_in_dim(wide_proj, part * local_width, local_width, 0)
    context_grad = matmul_right_t(attn_grad, proj_here).astype(LOW)
    query_grads, key_grads, value_grads = attention_backward(
        queries, keys, values, context_grad, logs
    )
    qkv_grad = jnp.concatenate([query_grads, key_grads, value_grads], axis=1)
    normed_one_grad = scatter_seq(matmul_right_t(qkv_grad, wide_qkv))
    _, norm_pull_one = jax.vjp(layer_norm, inputs_low.astype(F32), gain_one, bias_one)
    input_part, gain_one_term, bias_one_term = norm_pull_one(normed_one_grad)
    tokens_gradient = (middle_grad + input_part).astype(LOW)
    attn_cols = lax.dynamic_slice_in_dim(attn_grad, part * local_width, local_width, 1)
    output_term = matmul_left_t(activated, all_grads).astype(LOW)
    hidden_term = matmul_left_t(lowered_two, pre_grad).astype(LOW)
    proj_term = matmul_left_t(context, attn_cols).astype(LOW)
    qkv_term = matmul_left_t(lowered_one, qkv_grad).astype(LOW)
    first_terms = jnp.concatenate([output_term, hidden_term], axis=1)
    second_terms = jnp.concatenate([proj_term, qkv_term], axis=1)
    first_sum = lax.psum_scatter(first_terms, "dp", scatter_dimension=0, tiled=True)
    second_sum = lax.psum_scatter(second_terms, "dp", scatter_dimension=0, tiled=True)
    first_all = lax.all_gather(first_sum, "seq", axis=0)
    second_all = lax.all_gather(second_sum, "seq", axis=0)
    output_gradient = first_all[:, :, :width].reshape(parts * hidden_rows, width).astype(F32)
    hidden_gradient = (
        first_all[:, :, width:]
        .reshape(parts, model_rows, groups, hidden_rows)
        .transpose(1, 2, 0, 3)
        .reshape(model_rows, parts * hidden_here)
        .astype(F32)
    )
    proj_gradient = (
        second_all[:, :, :local_width].transpose(1, 0, 2).reshape(model_rows, width).astype(F32)
    )
    qkv_gradient = (
        second_all[:, :, local_width:]
        .reshape(parts, model_rows, 3, local_width)
        .transpose(1, 2, 0, 3)
        .reshape(model_rows, 3 * width)
        .astype(F32)
    )
    norm_terms = jnp.stack([gain_one_term, bias_one_term, gain_two_term, bias_two_term], axis=0)
    norm_sum = lax.psum(norm_terms, ("seq", "dp"))
    norm_own = lax.dynamic_slice_in_dim(
        norm_sum, lax.axis_index("dp") * first_gain.shape[0], first_gain.shape[0], 1
    )
    return (
        block_out.astype(LOW)[None],
        tokens_gradient[None],
        qkv_gradient,
        proj_gradient,
        hidden_gradient,
        output_gradient,
        norm_own[0],
        norm_own[1],
        norm_own[2],
        norm_own[3],
    )


def solution(mesh):
    placed = (
        P("dp", "seq", None),
        P("dp", None),
        P("dp", None),
        P("dp", None),
        P("dp", None),
        P("dp"),
        P("dp"),
        P("dp"),
        P("dp"),
        P("dp", "seq", None),
    )
    return jax.shard_map(
        on_device,
        mesh=mesh,
        in_specs=placed,
        out_specs=(
            P("dp", "seq", None),
            P("dp", "seq", None),
            P("dp", None),
            P("dp", None),
            P("dp", None),
            P("dp", None),
            P("dp"),
            P("dp"),
            P("dp"),
            P("dp"),
        ),
        check_vma=False,
    )
```

profile of v0, /device:TPU:0, one launch (start us, length us, event | category | flops | bytes accessed | tf_op | source)
XLA Modules:
  0.0 499.9 jit_solution(855848961846258834)
XLA Ops:
  10.8 10.3 %all-gather.4 = bf16[8,96,4]{1,2,0:T(4,128)(2,1)S(1)} all-gather(bf16[1,96,4]{1,2,0:T(4,128)(2,1)S(1)} %maximum_bitcast_fusion), channel_id=1, replica_groups=mesh['seq'=4,'dp'=8] {'dp'}, dimensions={0}, use_global_device_ids=true | all-gather | bytes 6912 | tf_op jit(solution)/shard_map/all_gather | solution.py:138
  24.7 11.9 %all_gather.41 = bf16[768,576]{1,0:T(8,128)(2,1)} all-gather(bf16[96,576]{1,0:T(8,128)(2,1)S(1)} %copy.126), channel_id=1, replica_groups=mesh['seq'=4,'dp'=8] {'dp'}, dimensions={0}, use_global_device_ids=true | all-gather | bytes 995328 | tf_op jit(solution)/shard_map/all_gather | solution.py:141
  36.7 13.9 %all-gather.24.cloned.1.call-done = bf16[1,1024,768]{1,2,0:T(8,128)(2,1)} async-done(((bf16[1,256,768]{1,2,0:T(8,128)(2,1)}), bf16[1,1024,768]{1,2,0:T(8,128)(2,1)}) %all-gather.24.cloned.1.call-update) | async-done | bytes 1572880 | tf_op jit(solution)/shard_map/all_gather | solution.py:35
  69.1 5.8 %all-gather.16.cloned.1.call-done = bf16[768,768]{1,0:T(8,128)(2,1)} async-done(((bf16[96,768]{1,0:T(8,128)(2,1)}), bf16[768,768]{1,0:T(8,128)(2,1)}) %all-gather.16.cloned.1.call-update) | async-done | bytes 1179664 | tf_op jit(solution)/shard_map/all_gather | solution.py:142
  74.8 39.3 %all-gather.14.cloned.1.call-done = bf16[1024,768]{0,1:T(8,128)(2,1)} async-done(((bf16[1024,192]{0,1:T(8,128)(2,1)}), bf16[1024,768]{0,1:T(8,128)(2,1)}) %all-gather.14.cloned.1.call-update) | async-done | bytes 1572880 | tf_op jit(solution)/shard_map/all_gather | solution.py:153
  114.1 3.7 fusion.90
  120.2 19.2 %all-gather.18.cloned.1.call-done = bf16[768,768]{1,0:T(8,128)(2,1)} async-done(((bf16[96,768]{1,0:T(8,128)(2,1)}), bf16[768,768]{1,0:T(8,128)(2,1)}) %all-gather.18.cloned.1.call-update) | async-done | bytes 1179664 | tf_op jit(solution)/shard_map/all_gather | solution.py:143
  139.4 4.8 fusion.91
  144.2 21.0 %all-gather.20.cloned.1.call-done = bf16[768,768]{1,0:T(8,128)(2,1)} async-done(((bf16[96,768]{1,0:T(8,128)(2,1)}), bf16[768,768]{1,0:T(8,128)(2,1)}) %all-gather.20.cloned.1.call-update) | async-done | bytes 1179664 | tf_op jit(solution)/shard_map/all_gather | solution.py:144
  165.2 38.5 %all-gather.26.cloned.1.call-done = bf16[1,1024,768]{2,1,0:T(8,128)(2,1)} async-done(((bf16[1,256,768]{2,1,0:T(8,128)(2,1)}), bf16[1,1024,768]{2,1,0:T(8,128)(2,1)}) %all-gather.26.cloned.1.call-update) | async-done | bytes 1572880 | tf_op jit(solution)/shard_map/all_gather | solution.py:35
  203.8 5.6 %fusion.16 = bf16[1024,768]{1,0:T(8,128)(2,1)S(1)} fusion(f32[1024,768]{1,0:T(8,128)} %fusion.91, bf16[768,768]{1,0:T(8,128)(2,1)} %all-gather.20.cloned.1.call-done, bf16[1,1024,768]{2,1,0:T(8,128)(2,1)} %all-gather.26.cloned.1.call-done), kind=kOutput, calls=%fused_computation.26 | convolution fusion | flops 1223688192 | bytes 7471104 | tf_op jit(solution)/shard_map/dot_general | solution.py:31
  210.5 2.6 convolution_convert_fusion.1
  213.4 3.5 convolution_convert_fusion.3
  220.2 4.3 copy.156
  227.2 20.3 %reduce-scatter.12.cloned.1.call-done = bf16[256,768]{0,1:T(8,128)(2,1)} async-done(((bf16[1024,768]{0,1:T(8,128)(2,1)}), bf16[256,768]{0,1:T(8,128)(2,1)}) %reduce-scatter.12.cloned.1.call-update) | async-done | bytes 393232 | tf_op jit(solution)/shard_map/reduce_scatter | solution.py:39
  247.5 2.0 multiply_reduce_fusion.3
  249.5 2.1 fusion.67
  252.2 2.7 fusion.70
  257.0 35.3 %reduce-scatter.18.cloned.1.call-done = bf16[96,1536]{1,0:T(8,128)(2,1)} async-done(((bf16[768,1536]{1,0:T(8,128)(2,1)}), bf16[96,1536]{1,0:T(8,128)(2,1)}) %reduce-scatter.18.cloned.1.call-update) | async-done | bytes 294928 | tf_op jit(solution)/shard_map/reduce_scatter | solution.py:186
  292.4 39.9 %all-gather.22.cloned.1.call-done = bf16[1024,768]{0,1:T(8,128)(2,1)} async-done(((bf16[256,768]{0,1:T(8,128)(2,1)}), bf16[1024,768]{0,1:T(8,128)(2,1)}) %all-gather.22.cloned.1.call-update) | async-done | bytes 1572880 | tf_op jit(solution)/shard_map/all_gather | solution.py:35
  332.3 2.0 convolution_convert_fusion.6
  351.5 2.5 convolution_convert_fusion
  354.3 5.0 %convolution_convert_fusion.2 = bf16[1024,768]{0,1:T(8,128)(2,1)} fusion(bf16[768,768]{1,0:T(8,128)(2,1)} %all-gather.20.cloned.1.call-done, f32[1024,768]{1,0:T(8,128)} %fusion.91), kind=kOutput, calls=%fused_computation.50 | convolution fusion | flops 1215823872 | bytes 5898240 | tf_op jit(solution)/shard_map/dot_general | solution.py:23
  362.5 2.4 fusion.84
  366.9 2.2 copy.143
  369.0 3.6 reshape.282
  373.8 28.3 %reduce-scatter.16.cloned.1.call-done = bf16[96,768]{1,0:T(8,128)(2,1)} async-done(((bf16[768,768]{1,0:T(8,128)(2,1)}), bf16[96,768]{1,0:T(8,128)(2,1)}) %reduce-scatter.16.cloned.1.call-update) | async-done | bytes 147472 | tf_op jit(solution)/shard_map/reduce_scatter | solution.py:187
  402.0 22.2 %all-gather.2 = bf16[384,768]{1,0:T(8,128)(2,1)S(1)} all-gather(bf16[96,768]{1,0:T(8,128)(2,1)} %reduce-scatter.16.cloned.1.call-done), channel_id=4, replica_groups=mesh['seq'=4,'dp'=8] {'seq'}, dimensions={0}, use_global_device_ids=true | all-gather | bytes 737280 | tf_op jit(solution)/shard_map/all_gather | solution.py:189
  427.8 2.9 reshape.280
  430.7 13.6 %reduce-scatter.14.cloned.1.call-done = bf16[256,768]{0,1:T(8,128)(2,1)} async-done(((bf16[1024,768]{0,1:T(8,128)(2,1)}), bf16[256,768]{0,1:T(8,128)(2,1)}) %reduce-scatter.14.cloned.1.call-update) | async-done | bytes 393232 | tf_op jit(solution)/shard_map/reduce_scatter | solution.py:39
  447.3 41.4 %psum.7 = f32[4,768]{1,0:T(4,128)S(1)} all-reduce(f32[4,768]{1,0:T(4,128)S(1)} %pad_maximum_fusion.6), channel_id=1, replica_groups=mesh['seq'=4,'dp'=8] {'seq','dp'}, use_global_device_ids=true, to_apply=%region_27.28 | all-reduce | flops 3072 | bytes 24576 | tf_op jit(solution)/shard_map/psum | solution.py:209
  489.3 2.0 fusion.73
  (228 shorter events, 70.0 us)
Async XLA Ops:
  7.2 60.5 %copy-start = (bf16[384,768]{1,0:T(8,128)(2,1)S(1)}, bf16[384,768]{1,0:T(8,128)(2,1)}, u32[]{:S(2)}) copy-start(bf16[384,768]{1,0:T(8,128)(2,1)} %param.14) | copy-start | bytes 1769476
  7.2 43.4 %all-gather.24.cloned.1.call-start = ((), (), s32[]{:S(2)}) async-start(), calls=%async_computation.13 | async-start | bytes 1966080 | tf_op jit(solution)/shard_map/all_gather | solution.py:35
  9.2 65.6 %all-gather.16.cloned.1.call-start = ((), (), s32[]{:S(2)}) async-start(), calls=%async_computation.6 | async-start | bytes 1327104 | tf_op jit(solution)/shard_map/all_gather | solution.py:142
  10.0 104.1 %all-gather.14.cloned.1.call-start = ((), (), s32[]{:S(2)}) async-start(), calls=%async_computation.5 | async-start | bytes 1966080 | tf_op jit(solution)/shard_map/all_gather | solution.py:153
  21.8 32.5 %copy-start.47 = (f32[768]{0:T(1024)}, f32[768]{0:T(1024)S(1)}, u32[]{:S(2)}) copy-start(f32[768]{0:T(1024)S(1)} %get-tuple-element.82) | copy-start | bytes 9220
  64.2 75.2 %all-gather.18.cloned.1.call-start = ((), (), s32[]{:S(2)}) async-start(), calls=%async_computation.7 | async-start | bytes 1327104 | tf_op jit(solution)/shard_map/all_gather | solution.py:143
  67.6 97.6 %all-gather.20.cloned.1.call-start = ((), (), s32[]{:S(2)}) async-start(), calls=%async_computation.8 | async-start | bytes 1327104 | tf_op jit(solution)/shard_map/all_gather | solution.py:144
  68.4 135.3 %all-gather.26.cloned.1.call-start = ((), (), s32[]{:S(2)}) async-start(), calls=%async_computation.14 | async-start | bytes 1966080 | tf_op jit(solution)/shard_map/all_gather | solution.py:35
  69.0 178.5 %reduce-scatter.12.cloned.1.call-start = ((), (), s32[]{:S(2)}) async-start(), calls=%async_computation.10 | async-start | bytes 1966080 | tf_op jit(solution)/shard_map/reduce_scatter | solution.py:39
  117.9 131.6 %copy-start.5 = (f32[1024,768]{0,1:T(8,128)}, f32[1024,768]{0,1:T(8,128)S(1)}, u32[]{:S(2)}) copy-start(f32[1024,768]{0,1:T(8,128)S(1)} %get-tuple-element.109) | copy-start | bytes 9437188
  203.8 6.8 %copy-start.53 = (bf16[768,768]{1,0:T(8,128)(2,1)S(1)}, bf16[768,768]{1,0:T(8,128)(2,1)}, u32[]{:S(2)}) copy-start(bf16[768,768]{1,0:T(8,128)(2,1)} %all-gather.18.cloned.1.call-done) | copy-start | bytes 3538948
  213.2 79.1 %reduce-scatter.18.cloned.1.call-start = ((), (), s32[]{:S(2)}) async-start(), calls=%async_computation.17 | async-start | bytes 2654208 | tf_op jit(solution)/shard_map/reduce_scatter | solution.py:186
  224.5 107.8 %all-gather.22.cloned.1.call-start = ((), (), s32[]{:S(2)}) async-start(), calls=%async_computation.11 | async-start | bytes 1966080 | tf_op jit(solution)/shard_map/all_gather | solution.py:35
  251.6 82.8 %copy-start.4 = (f32[3,512,512]{1,2,0:T(8,128)S(1)}, f32[3,512,512]{1,2,0:T(8,128)}, u32[]{:S(2)}) copy-start(f32[3,512,512]{1,2,0:T(8,128)} %copy-done.3) | copy-start | bytes 9437188
  254.9 107.6 %all-gather.28.cloned.1.call-start = ((), (), s32[]{:S(2)}) async-start(), calls=%async_computation.15 | async-start | bytes 1474560 | tf_op jit(solution)/shard_map/all_gather | solution.py:188
  292.3 109.7 %reduce-scatter.16.cloned.1.call-start = ((), (), s32[]{:S(2)}) async-start(), calls=%async_computation.16 | async-start | bytes 1327104 | tf_op jit(solution)/shard_map/reduce_scatter | solution.py:187
  337.4 10.9 %copy-start.26 = (bf16[3,64,512]{2,1,0:T(8,128)(2,1)}, bf16[3,64,512]{2,1,0:T(8,128)(2,1)S(1)}, u32[]{:S(2)}) copy-start(bf16[3,64,512]{2,1,0:T(8,128)(2,1)S(1)} %fusion.52) | copy-start | bytes 589828
  351.4 92.9 %reduce-scatter.14.cloned.1.call-start = ((), (), s32[]{:S(2)}) async-start(), calls=%async_computation.12 | async-start | bytes 1966080 | tf_op jit(solution)/shard_map/reduce_scatter | solution.py:39
  354.1 5.4 %copy-start.6 = (bf16[1,256,768]{1,2,0:T(8,128)(2,1)S(1)}, bf16[1,256,768]{1,2,0:T(8,128)(2,1)}, u32[]{:S(2)}) copy-start(bf16[1,256,768]{1,2,0:T(8,128)(2,1)} %copy.123) | copy-start | bytes 1179652
  354.1 6.0 %copy-start.34 = (f32[768]{0:T(1024)S(1)}, f32[768]{0:T(1024)}, u32[]{:S(2)}) copy-start(f32[768]{0:T(1024)} %get-tuple-element.79) | copy-start | bytes 9220
  354.1 6.6 %copy-start.35 = (f32[768]{0:T(1024)S(1)}, f32[768]{0:T(1024)}, u32[]{:S(2)}) copy-start(f32[768]{0:T(1024)} %get-tuple-element.70) | copy-start | bytes 9220
  354.1 135.2 %reduce-scatter.10.cloned.1.call-start = ((), (), s32[]{:S(2)}) async-start(), calls=%async_computation.9 | async-start | bytes 1966080 | tf_op jit(solution)/shard_map/reduce_scatter | solution.py:39
  426.1 18.2 %copy-start.38 = (f32[256]{0:T(256)S(1)}, f32[256]{0:T(256)}, u32[]{:S(2)}) copy-start(f32[256]{0:T(256)} %broadcast_multiply_fusion.2) | copy-start | bytes 3076
  426.1 21.1 %copy-start.43 = (f32[1,768]{1,0:T(1,128)S(1)}, f32[1,768]{1,0:T(1,128)}, u32[]{:S(2)}) copy-start(f32[1,768]{1,0:T(1,128)} %reshape.279) | copy-start | bytes 9220
  426.1 21.1 %copy-start.44 = (f32[1,768]{1,0:T(1,128)S(1)}, f32[1,768]{1,0:T(1,128)}, u32[]{:S(2)}) copy-start(f32[1,768]{1,0:T(1,128)} %reshape.278) | copy-start | bytes 9220
  426.2 63.1 %copy-start.9 = (bf16[256,768]{0,1:T(8,128)(2,1)S(1)}, bf16[256,768]{0,1:T(8,128)(2,1)}, u32[]{:S(2)}) copy-start(bf16[256,768]{0,1:T(8,128)(2,1)} %reduce-scatter.12.cloned.1.call-done) | copy-start | bytes 1179652
  426.2 63.1 %copy-start.10 = (bf16[1,256,768]{1,2,0:T(8,128)(2,1)S(1)}, bf16[1,256,768]{1,2,0:T(8,128)(2,1)}, u32[]{:S(2)}) copy-start(bf16[1,256,768]{1,2,0:T(8,128)(2,1)} %copy.130) | copy-start | bytes 1179652
  426.2 63.1 %copy-start.32 = (f32[256]{0:T(256)S(1)}, f32[256]{0:T(256)}, u32[]{:S(2)}) copy-start(f32[256]{0:T(256)} %broadcast_multiply_fusion.3) | copy-start | bytes 3076
  426.2 63.1 %copy-start.40 = (f32[256]{0:T(256)S(1)}, f32[256]{0:T(256)}, u32[]{:S(2)}) copy-start(f32[256]{0:T(256)} %copy-done.39) | copy-start | bytes 3076
  426.2 63.1 %copy-start.42 = (f32[256]{0:T(256)S(1)}, f32[256]{0:T(256)}, u32[]{:S(2)}) copy-start(f32[256]{0:T(256)} %copy-done.41) | copy-start | bytes 3076
  426.2 63.1 %copy-start.46 = (f32[256]{0:T(256)S(1)}, f32[256]{0:T(256)}, u32[]{:S(2)}) copy-start(f32[256]{0:T(256)} %copy-done.45) | copy-start | bytes 3076
  444.3 48.9 %copy-start.1 = (bf16[384,768]{1,0:T(8,128)(2,1)S(1)}, bf16[384,768]{1,0:T(8,128)(2,1)}, u32[]{:S(2)}) copy-start(bf16[384,768]{1,0:T(8,128)(2,1)} %param.14) | copy-start | bytes 1769476
  (39 other events, 92.1 us)
Sparse Core Ops, SparseCore 0:
  10.2 40.3 all-gather.23
  52.5 22.3 all-gather.15
  77.0 37.0 all-gather.13
  116.4 22.9 all-gather.17
  141.1 24.0 all-gather.19
  166.6 37.0 all-gather.25
  213.3 34.1 reduce-scatter.11
  250.8 41.4 reduce-scatter.17
  294.5 37.6 all-gather.21
  333.8 28.7 all-gather.27
  366.1 35.8 reduce-scatter.15
  404.2 40.0 reduce-scatter.13
  446.6 35.2 reduce-scatter.9
where the time goes:
time: 508 us; the launch traced here: 500 us
  waiting for transfers between devices  278 us (55%)
  blocking collectives  85.8 us (17%)
  matrix products  48.4 us (10%)
  local copies, waits for them, and re-layouts  38.9 us (8%)
  other arithmetic  32.6 us (6%)
  between operations  15.1 us (3%)
    all_gather x3, waiting for transfers between devices, gather_seq(): return lax.all_gather(value, 'seq', axis=0, tiled=True)  92.4 us
    psum x1, blocking collectives, on_device(): norm_sum = lax.psum(norm_terms, ('seq', 'dp'))  41.4 us
    all_gather x1, waiting for transfers between devices, on_device(): context = lax.all_gather(context_here, 'seq', axis=1, tiled=True)  39.3 us
    reduce_scatter x1, waiting for transfers between devices, on_device(): lax.psum_scatter(first_terms, 'dp', scatter_dimension=0, tiled=True)  35.3 us
    reduce_scatter x3, waiting for transfers between devices, scatter_seq(): lax.psum_scatter(value.astype(LOW), 'seq', scatter_dimension=0, tiled=True)  33.9 us
    reduce_scatter x1, waiting for transfers between devices, on_device(): lax.psum_scatter(second_terms, 'dp', scatter_dimension=0, tiled=True)  28.3 us
    all_gather x1, blocking collectives, on_device(): second_all = lax.all_gather(second_sum, 'seq', axis=0)  22.2 us
    all_gather x1, waiting for transfers between devices, on_device(): wide_output = lax.all_gather(output_here, 'dp', axis=0, tiled=True)  21 us
  transfers between devices with their start and end apart: 13, of which 12 were waited for; matrix products, arithmetic and copies ran while one was open for 20% of the time, Pallas kernels for 0%

commit v1 on v0

--- a/solution.py
+++ b/solution.py
@@ -138,8 +138,11 @@
     norms = lax.all_gather(norms, "dp", axis=1, tiled=True).astype(F32)
     gain_one, bias_one, gain_two, bias_two = (norms[0], norms[1], norms[2], norms[3])
     all_tokens = gather_seq(inputs_low)
-    wide_qkv = lax.all_gather(qkv_here, "dp", axis=0, tiled=True)
-    wide_proj = lax.all_gather(proj_weight, "dp", axis=0, tiled=True)
+    wide_qkv, wide_proj = jnp.split(
+        lax.all_gather(jnp.concatenate([qkv_here, proj_weight], axis=1), "dp", axis=0, tiled=True),
+        [qkv_here.shape[1]],
+        axis=1,
+    )
     wide_hidden = lax.all_gather(hidden_cols, "dp", axis=0, tiled=True)
     wide_output = lax.all_gather(output_here, "dp", axis=0, tiled=True)
     all_grads = gather_seq(cotangent[0])

time: 508 us -> 524 us (1.031)
  waiting for transfers between devices: 278 us -> 298 us
  blocking collectives: 85.8 us -> 73.9 us
    all_gather x1, waiting for transfers between devices: 5.78 us -> 25.2 us  [on_device(): lax.all_gather(jnp.concatenate([qkv_here, proj_weight], axis=1), 'dp', ax...]
    all_gather x1 -> x0, blocking collectives: 11.9 us -> none  [on_device(): wide_qkv = lax.all_gather(qkv_here, 'dp', axis=0, tiled=True)]
    all_gather x3, waiting for transfers between devices: 92.4 us -> 104 us  [gather_seq(): return lax.all_gather(value, 'seq', axis=0, tiled=True)]
    all_gather x1, waiting for transfers between devices: 39.3 us -> 32.5 us  [on_device(): context = lax.all_gather(context_here, 'seq', axis=1, tiled=True)]
    unnamed x123 -> x133, local copies, waits for them, and re-layouts: 16.8 us -> 18.3 us
  transfers between devices with their start and end apart: 13 -> 13, of which waited for: 12 -> 12; matrix products, arithmetic and copies ran while one was open for 20% -> 19% of each run, Pallas kernels for 0% -> 0%
where the time goes in v1:
time: 524 us; the launch traced here: 516 us
  waiting for transfers between devices  298 us (57%)
  blocking collectives  73.9 us (14%)
  matrix products  50.8 us (10%)
  local copies, waits for them, and re-layouts  43.5 us (8%)
  other arithmetic  32.8 us (6%)
  between operations  15.2 us (3%)
    all_gather x3, waiting for transfers between devices, gather_seq(): return lax.all_gather(value, 'seq', axis=0, tiled=True)  104 us
    psum x1, blocking collectives, on_device(): norm_sum = lax.psum(norm_terms, ('seq', 'dp'))  41.4 us
    reduce_scatter x3, waiting for transfers between devices, scatter_seq(): lax.psum_scatter(value.astype(LOW), 'seq', scatter_dimension=0, tiled=True)  33.9 us
    reduce_scatter x1, waiting for transfers between devices, on_device(): lax.psum_scatter(first_terms, 'dp', scatter_dimension=0, tiled=True)  32.8 us
    all_gather x1, waiting for transfers between devices, on_device(): context = lax.all_gather(context_here, 'seq', axis=1, tiled=True)  32.5 us
    reduce_scatter x1, waiting for transfers between devices, on_device(): lax.psum_scatter(second_terms, 'dp', scatter_dimension=0, tiled=True)  28.3 us
    all_gather x1, waiting for transfers between devices, on_device(): lax.all_gather(jnp.concatenate([qkv_here, proj_weight], axis=1), 'dp', ax...  25.2 us
    all_gather x1, blocking collectives, on_device(): second_all = lax.all_gather(second_sum, 'seq', axis=0)  22.2 us
  transfers between devices with their start and end apart: 13, of which 12 were waited for; matrix products, arithmetic and copies ran while one was open for 19% of the time, Pallas kernels for 0%

profile of v1, /device:TPU:0, one launch (start us, length us, event | category | flops | bytes accessed | tf_op | source)
XLA Modules:
  0.0 515.7 jit_solution(452102896286852603)
XLA Ops:
  7.3 2.0 copy.127
  12.7 10.3 %all-gather.4 = bf16[8,96,4]{1,2,0:T(4,128)(2,1)S(1)} all-gather(bf16[1,96,4]{1,2,0:T(4,128)(2,1)S(1)} %maximum_bitcast_fusion), channel_id=1, replica_groups=mesh['seq'=4,'dp'=8] {'dp'}, dimensions={0}, use_global_device_ids=true | all-gather | bytes 6912 | tf_op jit(solution)/shard_map/all_gather | solution.py:138
  25.0 25.6 %all-gather.24.cloned.1.call-done = bf16[1,1024,768]{1,2,0:T(8,128)(2,1)} async-done(((bf16[1,256,768]{1,2,0:T(8,128)(2,1)}), bf16[1,1024,768]{1,2,0:T(8,128)(2,1)}) %all-gather.24.cloned.1.call-update) | async-done | bytes 1572880 | tf_op jit(solution)/shard_map/all_gather | solution.py:35
  54.4 25.2 %all-gather.14.cloned.1.call-done = bf16[768,1344]{1,0:T(8,128)(2,1)} async-done(((bf16[96,1344]{1,0:T(8,128)(2,1)}), bf16[768,1344]{1,0:T(8,128)(2,1)}) %all-gather.14.cloned.1.call-update) | async-done | bytes 2064400 | tf_op jit(solution)/shard_map/all_gather | solution.py:142
  79.6 2.5 convolution_convert_fusion.4
  96.8 32.5 %all-gather.16.cloned.1.call-done = bf16[1024,768]{0,1:T(8,128)(2,1)} async-done(((bf16[1024,192]{0,1:T(8,128)(2,1)}), bf16[1024,768]{0,1:T(8,128)(2,1)}) %all-gather.16.cloned.1.call-update) | async-done | bytes 1572880 | tf_op jit(solution)/shard_map/all_gather | solution.py:156
  129.3 4.1 fusion.93
  135.8 18.8 %all-gather.18.cloned.1.call-done = bf16[768,768]{1,0:T(8,128)(2,1)} async-done(((bf16[96,768]{1,0:T(8,128)(2,1)}), bf16[768,768]{1,0:T(8,128)(2,1)}) %all-gather.18.cloned.1.call-update) | async-done | bytes 1179664 | tf_op jit(solution)/shard_map/all_gather | solution.py:146
  154.6 4.8 fusion.94
  159.4 21.6 %all-gather.20.cloned.1.call-done = bf16[768,768]{1,0:T(8,128)(2,1)} async-done(((bf16[96,768]{1,0:T(8,128)(2,1)}), bf16[768,768]{1,0:T(8,128)(2,1)}) %all-gather.20.cloned.1.call-update) | async-done | bytes 1179664 | tf_op jit(solution)/shard_map/all_gather | solution.py:147
  181.0 38.5 %all-gather.26.cloned.1.call-done = bf16[1,1024,768]{2,1,0:T(8,128)(2,1)} async-done(((bf16[1,256,768]{2,1,0:T(8,128)(2,1)}), bf16[1,1024,768]{2,1,0:T(8,128)(2,1)}) %all-gather.26.cloned.1.call-update) | async-done | bytes 1572880 | tf_op jit(solution)/shard_map/all_gather | solution.py:35
  219.5 5.6 %fusion.16 = bf16[1024,768]{1,0:T(8,128)(2,1)S(1)} fusion(f32[1024,768]{1,0:T(8,128)} %fusion.94, bf16[768,768]{1,0:T(8,128)(2,1)} %all-gather.20.cloned.1.call-done, bf16[1,1024,768]{2,1,0:T(8,128)(2,1)} %all-gather.26.cloned.1.call-done), kind=kOutput, calls=%fused_computation.26 | convolution fusion | flops 1223688192 | bytes 7471104 | tf_op jit(solution)/shard_map/dot_general | solution.py:31
  226.3 2.6 convolution_convert_fusion.1
  229.1 3.5 convolution_convert_fusion.3
  235.9 4.3 copy.160
  242.9 20.3 %reduce-scatter.12.cloned.1.call-done = bf16[256,768]{0,1:T(8,128)(2,1)} async-done(((bf16[1024,768]{0,1:T(8,128)(2,1)}), bf16[256,768]{0,1:T(8,128)(2,1)}) %reduce-scatter.12.cloned.1.call-update) | async-done | bytes 393232 | tf_op jit(solution)/shard_map/reduce_scatter | solution.py:39
  265.2 2.1 fusion.69
  267.9 2.2 fusion.72
  270.1 3.1 split.9
  275.2 32.8 %reduce-scatter.18.cloned.1.call-done = bf16[96,1536]{1,0:T(8,128)(2,1)} async-done(((bf16[768,1536]{1,0:T(8,128)(2,1)}), bf16[96,1536]{1,0:T(8,128)(2,1)}) %reduce-scatter.18.cloned.1.call-update) | async-done | bytes 294928 | tf_op jit(solution)/shard_map/reduce_scatter | solution.py:189
  308.3 39.7 %all-gather.22.cloned.1.call-done = bf16[1024,768]{0,1:T(8,128)(2,1)} async-done(((bf16[256,768]{0,1:T(8,128)(2,1)}), bf16[1024,768]{0,1:T(8,128)(2,1)}) %all-gather.22.cloned.1.call-update) | async-done | bytes 1572880 | tf_op jit(solution)/shard_map/all_gather | solution.py:35
  348.0 2.0 convolution_convert_fusion.6
  367.2 3.8 convolution_convert_fusion
  371.4 4.6 convolution_convert_fusion.2
  378.2 2.4 fusion.87
  382.6 2.2 copy.147
  384.7 3.6 reshape.282
  389.5 28.3 %reduce-scatter.16.cloned.1.call-done = bf16[96,768]{1,0:T(8,128)(2,1)} async-done(((bf16[768,768]{1,0:T(8,128)(2,1)}), bf16[96,768]{1,0:T(8,128)(2,1)}) %reduce-scatter.16.cloned.1.call-update) | async-done | bytes 147472 | tf_op jit(solution)/shard_map/reduce_scatter | solution.py:190
  417.8 22.2 %all-gather.2 = bf16[384,768]{1,0:T(8,128)(2,1)S(1)} all-gather(bf16[96,768]{1,0:T(8,128)(2,1)} %reduce-scatter.16.cloned.1.call-done), channel_id=4, replica_groups=mesh['seq'=4,'dp'=8] {'seq'}, dimensions={0}, use_global_device_ids=true | all-gather | bytes 737280 | tf_op jit(solution)/shard_map/all_gather | solution.py:192
  443.5 2.9 reshape.280
  446.4 13.6 %reduce-scatter.14.cloned.1.call-done = bf16[256,768]{0,1:T(8,128)(2,1)} async-done(((bf16[1024,768]{0,1:T(8,128)(2,1)}), bf16[256,768]{0,1:T(8,128)(2,1)}) %reduce-scatter.14.cloned.1.call-update) | async-done | bytes 393232 | tf_op jit(solution)/shard_map/reduce_scatter | solution.py:39
  463.0 41.4 %psum.7 = f32[4,768]{1,0:T(4,128)S(1)} all-reduce(f32[4,768]{1,0:T(4,128)S(1)} %pad_maximum_fusion.7), channel_id=1, replica_groups=mesh['seq'=4,'dp'=8] {'seq','dp'}, use_global_device_ids=true, to_apply=%region_27.28 | all-reduce | flops 3072 | bytes 24576 | tf_op jit(solution)/shard_map/psum | solution.py:212
  (239 shorter events, 71.5 us)
Async XLA Ops:
  7.2 88.3 %copy-start = (bf16[384,768]{1,0:T(8,128)(2,1)S(1)}, bf16[384,768]{1,0:T(8,128)(2,1)}, u32[]{:S(2)}) copy-start(bf16[384,768]{1,0:T(8,128)(2,1)} %param.14) | copy-start | bytes 1769476
  7.2 43.4 %all-gather.24.cloned.1.call-start = ((), (), s32[]{:S(2)}) async-start(), calls=%async_computation.13 | async-start | bytes 1966080 | tf_op jit(solution)/shard_map/all_gather | solution.py:35
  9.3 70.2 %all-gather.14.cloned.1.call-start = ((), (), s32[]{:S(2)}) async-start(), calls=%async_computation.5 | async-start | bytes 2433024 | tf_op jit(solution)/shard_map/all_gather | solution.py:142
  12.6 116.8 %all-gather.16.cloned.1.call-start = ((), (), s32[]{:S(2)}) async-start(), calls=%async_computation.6 | async-start | bytes 1966080 | tf_op jit(solution)/shard_map/all_gather | solution.py:156
  23.7 55.8 %copy-start.47 = (f32[768]{0:T(1024)}, f32[768]{0:T(1024)S(1)}, u32[]{:S(2)}) copy-start(f32[768]{0:T(1024)S(1)} %get-tuple-element.82) | copy-start | bytes 9220
  50.7 28.9 %copy-start.7 = (bf16[1,1024,768]{1,2,0:T(8,128)(2,1)S(1)}, bf16[1,1024,768]{1,2,0:T(8,128)(2,1)}, u32[]{:S(2)}) copy-start(bf16[1,1024,768]{1,2,0:T(8,128)(2,1)} %all-gather.24.cloned.1.call-done) | copy-start | bytes 4718596
  52.5 29.6 %copy-start.36 = (f32[1024]{0:T(1024)}, f32[1024]{0:T(1024)S(1)}, u32[]{:S(2)}) copy-start(f32[1024]{0:T(1024)S(1)} %broadcast_multiply_fusion.1) | copy-start | bytes 12292
  54.3 25.2 %copy-start.49 = (f32[1024]{0:T(1024)}, f32[1024]{0:T(1024)S(1)}, u32[]{:S(2)}) copy-start(f32[1024]{0:T(1024)S(1)} %add_rsqrt_fusion.1) | copy-start | bytes 12292
  92.0 62.5 %all-gather.18.cloned.1.call-start = ((), (), s32[]{:S(2)}) async-start(), calls=%async_computation.7 | async-start | bytes 1327104 | tf_op jit(solution)/shard_map/all_gather | solution.py:146
  95.5 85.5 %all-gather.20.cloned.1.call-start = ((), (), s32[]{:S(2)}) async-start(), calls=%async_computation.8 | async-start | bytes 1327104 | tf_op jit(solution)/shard_map/all_gather | solution.py:147
  96.2 123.3 %all-gather.26.cloned.1.call-start = ((), (), s32[]{:S(2)}) async-start(), calls=%async_computation.14 | async-start | bytes 1966080 | tf_op jit(solution)/shard_map/all_gather | solution.py:35
  96.8 166.4 %reduce-scatter.12.cloned.1.call-start = ((), (), s32[]{:S(2)}) async-start(), calls=%async_computation.10 | async-start | bytes 1966080 | tf_op jit(solution)/shard_map/reduce_scatter | solution.py:39
  133.4 133.9 %copy-start.5 = (f32[1024,768]{0,1:T(8,128)}, f32[1024,768]{0,1:T(8,128)S(1)}, u32[]{:S(2)}) copy-start(f32[1024,768]{0,1:T(8,128)S(1)} %get-tuple-element.109) | copy-start | bytes 9437188
  219.5 6.8 %copy-start.58 = (bf16[768,768]{1,0:T(8,128)(2,1)S(1)}, bf16[768,768]{1,0:T(8,128)(2,1)}, u32[]{:S(2)}) copy-start(bf16[768,768]{1,0:T(8,128)(2,1)} %all-gather.18.cloned.1.call-done) | copy-start | bytes 3538948
  228.9 79.2 %reduce-scatter.18.cloned.1.call-start = ((), (), s32[]{:S(2)}) async-start(), calls=%async_computation.17 | async-start | bytes 2654208 | tf_op jit(solution)/shard_map/reduce_scatter | solution.py:189
  240.2 107.8 %all-gather.22.cloned.1.call-start = ((), (), s32[]{:S(2)}) async-start(), calls=%async_computation.11 | async-start | bytes 1966080 | tf_op jit(solution)/shard_map/all_gather | solution.py:35
  270.0 80.0 %copy-start.4 = (f32[3,512,512]{1,2,0:T(8,128)S(1)}, f32[3,512,512]{1,2,0:T(8,128)}, u32[]{:S(2)}) copy-start(f32[3,512,512]{1,2,0:T(8,128)} %copy-done.3) | copy-start | bytes 9437188
  270.1 108.2 %all-gather.28.cloned.1.call-start = ((), (), s32[]{:S(2)}) async-start(), calls=%async_computation.15 | async-start | bytes 1474560 | tf_op jit(solution)/shard_map/all_gather | solution.py:191
  308.1 109.7 %reduce-scatter.16.cloned.1.call-start = ((), (), s32[]{:S(2)}) async-start(), calls=%async_computation.16 | async-start | bytes 1327104 | tf_op jit(solution)/shard_map/reduce_scatter | solution.py:190
  353.1 10.9 %copy-start.25 = (bf16[3,64,512]{2,1,0:T(8,128)(2,1)}, bf16[3,64,512]{2,1,0:T(8,128)(2,1)S(1)}, u32[]{:S(2)}) copy-start(bf16[3,64,512]{2,1,0:T(8,128)(2,1)S(1)} %fusion.52) | copy-start | bytes 589828
  367.2 92.8 %reduce-scatter.14.cloned.1.call-start = ((), (), s32[]{:S(2)}) async-start(), calls=%async_computation.12 | async-start | bytes 1966080 | tf_op jit(solution)/shard_map/reduce_scatter | solution.py:39
  371.1 133.9 %reduce-scatter.10.cloned.1.call-start = ((), (), s32[]{:S(2)}) async-start(), calls=%async_computation.9 | async-start | bytes 1966080 | tf_op jit(solution)/shard_map/reduce_scatter | solution.py:39
  441.8 18.2 %copy-start.38 = (f32[256]{0:T(256)S(1)}, f32[256]{0:T(256)}, u32[]{:S(2)}) copy-start(f32[256]{0:T(256)} %broadcast_multiply_fusion.2) | copy-start | bytes 3076
  441.8 21.2 %copy-start.43 = (f32[1,768]{1,0:T(1,128)S(1)}, f32[1,768]{1,0:T(1,128)}, u32[]{:S(2)}) copy-start(f32[1,768]{1,0:T(1,128)} %reshape.279) | copy-start | bytes 9220
  441.8 21.2 %copy-start.44 = (f32[1,768]{1,0:T(1,128)S(1)}, f32[1,768]{1,0:T(1,128)}, u32[]{:S(2)}) copy-start(f32[1,768]{1,0:T(1,128)} %reshape.278) | copy-start | bytes 9220
  441.9 63.2 %copy-start.9 = (bf16[256,768]{0,1:T(8,128)(2,1)S(1)}, bf16[256,768]{0,1:T(8,128)(2,1)}, u32[]{:S(2)}) copy-start(bf16[256,768]{0,1:T(8,128)(2,1)} %reduce-scatter.12.cloned.1.call-done) | copy-start | bytes 1179652
  441.9 63.1 %copy-start.10 = (bf16[1,256,768]{1,2,0:T(8,128)(2,1)S(1)}, bf16[1,256,768]{1,2,0:T(8,128)(2,1)}, u32[]{:S(2)}) copy-start(bf16[1,256,768]{1,2,0:T(8,128)(2,1)} %copy.134) | copy-start | bytes 1179652
  441.9 63.1 %copy-start.32 = (f32[256]{0:T(256)S(1)}, f32[256]{0:T(256)}, u32[]{:S(2)}) copy-start(f32[256]{0:T(256)} %broadcast_multiply_fusion.3) | copy-start | bytes 3076
  441.9 63.1 %copy-start.40 = (f32[256]{0:T(256)S(1)}, f32[256]{0:T(256)}, u32[]{:S(2)}) copy-start(f32[256]{0:T(256)} %copy-done.39) | copy-start | bytes 3076
  441.9 63.1 %copy-start.42 = (f32[256]{0:T(256)S(1)}, f32[256]{0:T(256)}, u32[]{:S(2)}) copy-start(f32[256]{0:T(256)} %copy-done.41) | copy-start | bytes 3076
  441.9 63.1 %copy-start.46 = (f32[256]{0:T(256)S(1)}, f32[256]{0:T(256)}, u32[]{:S(2)}) copy-start(f32[256]{0:T(256)} %copy-done.45) | copy-start | bytes 3076
  460.0 48.9 %copy-start.1 = (bf16[384,768]{1,0:T(8,128)(2,1)S(1)}, bf16[384,768]{1,0:T(8,128)(2,1)}, u32[]{:S(2)}) copy-start(bf16[384,768]{1,0:T(8,128)(2,1)} %param.14) | copy-start | bytes 1769476
  (44 other events, 123.4 us)
Sparse Core Ops, SparseCore 0:
  10.2 40.3 all-gather.23
  53.1 26.4 all-gather.13
  92.2 37.0 all-gather.15
  131.6 22.9 all-gather.17
  156.9 24.0 all-gather.19
  182.4 37.0 all-gather.25
  229.0 34.1 reduce-scatter.11
  266.6 41.4 reduce-scatter.17
  310.3 37.6 all-gather.21
  349.5 28.7 all-gather.27
  381.8 35.8 reduce-scatter.15
  419.9 40.0 reduce-scatter.13
  462.3 35.2 reduce-scatter.9
